TPU v7x, 512 devices: a whole 4x8x8 slice. The times are simulated.
512 devices in a mesh: row: 32 (over y_hi, z), col: 16 (over y_lo, x, core).
Axes of the slice: x: 4, y: 8 (y_hi: 4, y_lo: 2; y = y_hi * 2 + y_lo), z: 8, core: 2. Of those that a mesh axis runs over, the one named last changes fastest.
Arguments:
- features: bfloat16 [65536, 256], P(('col', 'row')), may hold values from -6 to 6
- weight: bfloat16 [256, 256], replicated, may hold values from -0.375 to 0.375
- cotangent: bfloat16 [65536, 256], P(('row', 'col')), may hold values from -6 to 6
- degrees: int32 [65536], replicated, may hold values from 0 to 63
- adj_blocks: bfloat16 [32, 16, 128, 128, 128], P('row', 'col'), may hold values from 0 to 0.046875
- block_rows: int32 [32, 16, 128], P('row', 'col'), may hold values from 0 to 15, as said below
- block_cols: int32 [32, 16, 128], P('row', 'col'), may hold values from 0 to 31
- block_count: int32 [32, 16], P('row', 'col'), may hold values from 16 to 128, as said below
Outputs:
- activations: bfloat16 [65536, 256], P(('row', 'col'))
- feature_grad: bfloat16 [65536, 256], P(('col', 'row'))
- weight_grad: float32 [256, 256], replicated
Inputs may be any that keep to these rules, and one draw needn't show every extreme that they name: Within one tile the pairs (block_rows, block_cols) of its 128 slots are all different. `block_count`: every tile whose first row node lies in its column range uses all 128 slots.
All inputs are finite; a program needn't handle non-finite values.
Results may differ from a plain program's by a relative error of at most 0.027.
Values may be sent and summed in bfloat16 or wider, within the bound.
A program may use at most 64 MiB of HBM per device.

v0:
```python
from functools import partial
import math

import jax
import jax.numpy as jnp
from jax import lax
from jax.sharding import PartitionSpec as P


def degree_scale(degrees):
    safe = jnp.maximum(degrees, 1).astype(jnp.float32)
    return jnp.where(degrees > 0, lax.rsqrt(safe), jnp.float32(0.0))


def accumulate(blocks, slot_index, targets, source, count, pattern, target_total, first):
    block_size = blocks.shape[-1]
    slot_total = blocks.shape[0]
    feat_width = source.shape[1]
    pieces = source.reshape(-1, block_size, feat_width)
    group_size = math.gcd(slot_total, 16)

    def add_group(group_index, totals):
        offset = group_index * group_size
        slab = lax.dynamic_slice_in_dim(blocks, offset, group_size, 0)
        picked = pieces[lax.dynamic_slice_in_dim(slot_index, offset, group_size, 0)]
        result = jnp.einsum(pattern, slab, picked, preferred_element_type=jnp.float32)
        dest = lax.dynamic_slice_in_dim(targets, offset, group_size, 0) - first
        live = (offset + jnp.arange(group_size) < count) & (dest >= 0) & (dest < target_total)
        dest = jnp.where(live, dest, target_total)
        return totals.at[dest].add(result, mode="drop")

    zeros_buffer = jnp.zeros((target_total, block_size, feat_width), jnp.float32)
    upper = slot_total // group_size
    totals = lax.fori_loop(0, upper, add_group, zeros_buffer)
    return totals.reshape(-1, feat_width)


def per_device(
    features, weight, cotangent, degrees, adj_blocks, block_rows, block_cols, block_count
):
    local_rows = features.shape[0]
    row_count = lax.axis_size("row")
    col_count = lax.axis_size("col")
    row_index = lax.axis_index("row")
    col_index = lax.axis_index("col")
    blocks = adj_blocks[0, 0]
    brows = block_rows[0, 0]
    bcols = block_cols[0, 0]
    count = block_count[0, 0]
    block_size = blocks.shape[-1]
    row_blocks = local_rows * col_count // block_size
    col_blocks = local_rows * row_count // block_size
    own_degrees = lax.dynamic_slice_in_dim(
        degrees, (col_index * row_count + row_index) * local_rows, local_rows
    )
    own_scale = degree_scale(own_degrees)
    row_degrees = lax.dynamic_slice_in_dim(
        degrees, (row_index * col_count + col_index) * local_rows, local_rows
    )
    row_scale = degree_scale(row_degrees)
    scaled = (features.astype(jnp.float32) * own_scale[:, None]).astype(jnp.bfloat16)
    col_source = lax.all_gather(scaled, "row", axis=0, tiled=True)
    forward_term = accumulate(
        blocks, bcols, brows, col_source, count, "kab,kbf->kaf", row_blocks, 0
    )
    summed = lax.psum_scatter(
        forward_term.astype(jnp.bfloat16), "col", scatter_dimension=0, tiled=True
    ).astype(jnp.float32)
    propagated = (summed * row_scale[:, None]).astype(jnp.bfloat16)
    pre = jnp.dot(propagated, weight, preferred_element_type=jnp.float32)
    output, backward = jax.vjp(partial(jax.nn.gelu, approximate=True), pre)
    activations = output.astype(jnp.bfloat16)
    pre_grad = backward(cotangent.astype(jnp.float32))[0].astype(jnp.bfloat16)
    local_wgrad = lax.dot_general(
        propagated, pre_grad, (((0,), (0,)), ((), ())), preferred_element_type=jnp.float32
    )
    weight_grad = lax.psum(local_wgrad, ("row", "col"))
    back_full = lax.dot_general(
        pre_grad, weight, (((1,), (1,)), ((), ())), preferred_element_type=jnp.float32
    )
    back_scaled = (back_full * row_scale[:, None]).astype(jnp.bfloat16)
    row_source = lax.all_gather(back_scaled, "col", axis=0, tiled=True)
    back_term = accumulate(blocks, brows, bcols, row_source, count, "kba,kbf->kaf", col_blocks, 0)
    back_sum = lax.psum_scatter(
        back_term.astype(jnp.bfloat16), "row", scatter_dimension=0, tiled=True
    ).astype(jnp.float32)
    feature_grad = (back_sum * own_scale[:, None]).astype(jnp.bfloat16)
    return (activations, feature_grad, weight_grad)


def solution(mesh):
    in_specs = (
        P(("col", "row"), None),
        P(),
        P(("row", "col"), None),
        P(),
        P("row", "col", None, None, None),
        P("row", "col", None),
        P("row", "col", None),
        P("row", "col"),
    )
    out_specs = (P(("row", "col"), None), P(("col", "row"), None), P())
    return jax.shard_map(
        per_device, mesh=mesh, in_specs=in_specs, out_specs=out_specs, check_vma=False
    )
```

profile of v0, /device:TPU:1, one launch (start us, length us, event | category | flops | bytes accessed | tf_op | source)
XLA Modules:
  0.0 858.1 jit_solution(13833930867638481680)
XLA Ops:
  9.7 92.0 %all-gather.3.cloned.1.call-done = bf16[4096,256]{1,0:T(8,128)(2,1)} async-done(((bf16[128,256]{1,0:T(8,128)(2,1)}), bf16[4096,256]{1,0:T(8,128)(2,1)}) %all-gather.3.cloned.1.call-update) | async-done | bytes 2097168 | tf_op jit(solution)/shard_map/all_gather | solution.py:62
  103.3 69.8 %while.26 = (s32[]{:T(128)}, f32[16,128,256]{2,1,0:T(8,128)}, s32[]{:T(128)}, s32[128]{0:T(128)S(1)}, bf16[128,128,128]{2,1,0:T(8,128)(2,1)}, /*index=5*/s32[128...) while((s32[]{:T(128)}, f32[16,128,256]{2,1,0:T(8,128)}, ...), condition=%wide.region_2.3_spmd, body=%wide.region_0.2_spmd.sunk | while | flops 134743248 | bytes 12063347 | solution.py:34
  107.7 4.3 scatter_fusion
  116.4 4.3 scatter_fusion
  125.1 4.3 scatter_fusion
  133.9 4.3 scatter_fusion
  142.6 4.3 scatter_fusion
  151.3 4.3 scatter_fusion
  160.0 4.3 scatter_fusion
  168.7 4.3 scatter_fusion
  175.8 62.2 %reduce-scatter.3.cloned.1.call-done = bf16[128,256]{1,0:T(8,128)(2,1)} async-done(((bf16[2048,256]{1,0:T(8,128)(2,1)}), bf16[128,256]{1,0:T(8,128)(2,1)}) %reduce-scatter.3.cloned.1.call-update) | async-done | bytes 65552 | tf_op jit(solution)/shard_map/reduce_scatter | solution.py:66
  240.7 6.4 copy.11
  247.1 32.8 %all-gather.5.cloned.1.call-done = bf16[2048,256]{1,0:T(8,128)(2,1)} async-done(((bf16[128,256]{1,0:T(8,128)(2,1)}), bf16[2048,256]{1,0:T(8,128)(2,1)}) %all-gather.5.cloned.1.call-update) | async-done | bytes 1048592 | tf_op jit(solution)/shard_map/all_gather | solution.py:82
  282.3 67.3 %while.27 = (s32[]{:T(128)}, f32[32,128,256]{2,1,0:T(8,128)}, s32[]{:T(128)}, s32[128]{0:T(128)S(1)}, bf16[128,128,128]{1,2,0:T(8,128)(2,1)}, /*index=5*/s32[128...) while((s32[]{:T(128)}, f32[32,128,256]{2,1,0:T(8,128)}, ...), condition=%wide.region_6.7_spmd, body=%wide.region_4.6_spmd.sunk | while | flops 134743248 | bytes 12063347 | solution.py:34
  286.4 4.5 scatter_fusion.1
  294.9 4.4 scatter_fusion.1
  303.4 4.5 scatter_fusion.1
  311.9 4.3 scatter_fusion.1
  320.2 4.3 scatter_fusion.1
  328.6 4.3 scatter_fusion.1
  336.9 4.3 scatter_fusion.1
  345.3 4.3 scatter_fusion.1
  355.2 221.0 %reduce-scatter.5.cloned.1.call-done = bf16[128,256]{1,0:T(8,128)(2,1)} async-done(((bf16[4096,256]{1,0:T(8,128)(2,1)}), bf16[128,256]{1,0:T(8,128)(2,1)}) %reduce-scatter.5.cloned.1.call-update) | async-done | bytes 65552 | tf_op jit(solution)/shard_map/reduce_scatter | solution.py:84
  577.8 272.1 %all-reduce.2.cloned.1.call-done = f32[256,256]{1,0:T(8,128)} async-done(((f32[256,256]{1,0:T(8,128)}), f32[256,256]{1,0:T(8,128)}) %all-reduce.2.cloned.1.call-update) | async-done | bytes 262160 | tf_op jit(solution)/shard_map/psum | solution.py:77
  (95 shorter events, 88.3 us)
Async XLA Ops:
  7.2 230.8 %copy-start = (bf16[256,256]{1,0:T(8,128)(2,1)S(1)}, bf16[256,256]{1,0:T(8,128)(2,1)}, u32[]{:S(2)}) copy-start(bf16[256,256]{1,0:T(8,128)(2,1)} %param.13) | copy-start | bytes 393220
  7.2 96.1 %copy-start.1 = (s32[1,1,128]{2,1,0:T(1,128)S(1)}, s32[1,1,128]{2,1,0:T(1,128)}, u32[]{:S(2)}) copy-start(s32[1,1,128]{2,1,0:T(1,128)} %param.17) | copy-start | bytes 1540
  7.2 96.1 %copy-start.2 = (s32[1,1,128]{2,1,0:T(1,128)S(1)}, s32[1,1,128]{2,1,0:T(1,128)}, u32[]{:S(2)}) copy-start(s32[1,1,128]{2,1,0:T(1,128)} %param.18) | copy-start | bytes 1540
  7.2 94.5 %all-gather.3.cloned.1.call-start = ((), (), s32[]{:S(2)}) async-start(), calls=%async_computation.2 | async-start | bytes 2162688 | tf_op jit(solution)/shard_map/all_gather | solution.py:62
  9.6 228.4 %reduce-scatter.3.cloned.1.call-start = ((), (), s32[]{:S(2)}) async-start(), calls=%async_computation.3 | async-start | bytes 1114112 | tf_op jit(solution)/shard_map/reduce_scatter | solution.py:66
  173.0 66.7 %copy-start.3 = (bf16[128,256]{1,0:T(8,128)(2,1)S(1)}, bf16[128,256]{1,0:T(8,128)(2,1)}, u32[]{:S(2)}) copy-start(bf16[128,256]{1,0:T(8,128)(2,1)} %param.14) | copy-start | bytes 196612
  175.8 104.1 %all-gather.5.cloned.1.call-start = ((), (), s32[]{:S(2)}) async-start(), calls=%async_computation.4 | async-start | bytes 1114112 | tf_op jit(solution)/shard_map/all_gather | solution.py:82
  240.6 335.6 %reduce-scatter.5.cloned.1.call-start = ((), (), s32[]{:S(2)}) async-start(), calls=%async_computation.5 | async-start | bytes 2162688 | tf_op jit(solution)/shard_map/reduce_scatter | solution.py:84
  353.4 0.8 copy-start.4
  353.4 496.5 %all-reduce.2.cloned.1.call-start = ((), (), s32[]{:S(2)}) async-start(), calls=%async_computation.6 | async-start | bytes 524288 | tf_op jit(solution)/shard_map/psum | solution.py:77
Sparse Core Ops, SparseCore 0:
  11.8 89.8 all-gather.2
  175.9 62.0 reduce-scatter.2
  241.0 38.8 all-gather.4
  353.5 222.6 reduce-scatter.4
  581.6 268.2 all-reduce.1
where the time goes:
time: 861 us; the launch traced here: 858 us
  waiting for transfers between devices  680 us (79%)
  other arithmetic  91.2 us (11%)
  local copies, waits for them, and re-layouts  45.2 us (5%)
  matrix products  27 us (3%)
  between operations  13.8 us (2%)
    psum x1, waiting for transfers between devices, per_device(): weight_grad = lax.psum(local_wgrad, ('row', 'col'))  272 us
    reduce_scatter x1, waiting for transfers between devices, per_device(): lax.psum_scatter(back_term.astype(jnp.bfloat16), 'row', scatter_dimension...  221 us
    all_gather x1, waiting for transfers between devices, per_device(): col_source = lax.all_gather(scaled, 'row', axis=0, tiled=True)  92 us
    scatter-add x16, other arithmetic, add_group(): return totals.at[dest].add(result, mode='drop')  69.1 us
    reduce_scatter x1, waiting for transfers between devices, per_device(): lax.psum_scatter(forward_term.astype(jnp.bfloat16), 'col', scatter_dimens...  62.2 us
    all_gather x1, waiting for transfers between devices, per_device(): row_source = lax.all_gather(back_scaled, 'col', axis=0, tiled=True)  32.8 us
    gather x16, local copies, waits for them, and re-layouts, add_group(): picked = pieces[lax.dynamic_slice_in_dim(slot_index, offset, group_size, 0)]  32.3 us
    dot_general x16, matrix products, add_group(): jnp.einsum(pattern, slab, picked, preferred_element_type=jnp.float32)  23.5 us
  transfers between devices with their start and end apart: 5, of which 5 were waited for; matrix products, arithmetic and copies ran while one was open for 1% of the time, Pallas kernels for 0%

commit v1 on v0

v1 whole, which is shorter than its diff:
```python
import math

import jax
import jax.numpy as jnp
from jax import lax
from jax.experimental import pallas as pl
from jax.experimental.pallas import tpu as pltpu
from jax.sharding import PartitionSpec as P

NY, NZ = 4, 8
NX, NL = 4, 2
CHIPS = NX * NL
BS = 128
F = 256
CAP = 128
BF, F32, I32 = jnp.bfloat16, jnp.float32, jnp.int32
MESH = pl.DeviceIdType.MESH

GELU_A = math.sqrt(2.0 / math.pi)
GELU_B = 0.044715

GATHER_ORDER = (0, 1, 3, 2)
SCATTER_ORDER = (2, 1, 3, 0)
CHIP_ORDER = ((1, 2), (1, 1), (1, 3), (1, 0), (0, 2), (0, 1), (0, 3), (0, 0))


def scale_of(degrees):
    safe = jnp.maximum(degrees, 1).astype(F32)
    return jnp.where(degrees > 0, lax.rsqrt(safe), jnp.float32(0.0))


def down_rows(line, width):
    square = jnp.broadcast_to(line, (BS, BS)).T
    return jnp.concatenate([square] * (width // BS), axis=1) if width > BS else square


def gather_has(way, step, d):
    return step < 3 or (step == 3 and (d in (0, 1)) == (way == 0))


def scatter_has(way, step, d):
    return step > 0 or (d in (2, 0)) == (way == 0)


def kernel(
    feat, weight, cot, deg, adj, brow, bcol, cnt,
    act_out, fg_out, wg_out,
    blocks, turned, src, acc, inv_v, inv_s,
    pair_out, pair_in, chip_out, chip_in, grads,
    part, ring_out, ring_in, last_out, last_in,
    w_half_out, w_half_in, w_piece_out, w_piece_in, w_z, w_y, w_all, w_other,
    adj_sem, inv_sem, gy_s, gy_r, gz_s, gz_r, pair_s, pair_r, chip_s, chip_r,
    ag_s, ag_r, fw_s, fw_r, rz_s, rz_r, ry_s, ry_r,
    wh_s, wh_r, wp_s, wp_r, wz_s, wz_r, wy_s, wy_r, wa_s, wa_r, wo_s, wo_r,
):
    row = lax.axis_index("row")
    col = lax.axis_index("col")
    y, z = row // NZ, row % NZ
    chip, core = col // 2, col % 2
    ylo, x = chip // NX, chip % NX

    def at_z(k):
        return (y * NZ + (z + k + NZ) % NZ, col)

    def at_y(d):
        return (((y + d) % NY) * NZ + z, col)

    def chip_at(k):
        dl, dx = CHIP_ORDER[k]
        return ((ylo + dl) % NL) * NX + (x + dx) % NX

    def chip_from(k):
        dl, dx = CHIP_ORDER[k]
        return ((ylo + NL - dl) % NL) * NX + (x + NX - dx) % NX

    def at_chip(k):
        return (row, chip_at(k) * 2 + core)

    sibling = (row, chip * 2 + 1 - core)

    adj_copy = pltpu.make_async_copy(adj, blocks.at[pl.ds(0, CAP)], adj_sem)
    adj_copy.start()

    barrier = pltpu.get_barrier_semaphore()
    partners = [at_z(k) for k in range(1, NZ)] + [at_y(d) for d in range(1, NY)]
    partners += [at_chip(k) for k in range(CHIPS - 1)] + [sibling]
    for partner in partners:
        pl.semaphore_signal(barrier, inc=1, device_id=partner, device_id_type=MESH)

    own_scale = down_rows(scale_of(deg[pl.ds(col * (NY * NZ) + row, 1), :]), F)
    src[row] = (feat[...].astype(F32) * own_scale).astype(BF)

    pl.semaphore_wait(barrier, len(partners))

    started = []

    def send(source, target, send_sem, recv_sem, device):
        copy = pltpu.make_async_remote_copy(
            src_ref=source, dst_ref=target, send_sem=send_sem, recv_sem=recv_sem,
            device_id=device, device_id_type=MESH,
        )
        copy.start()
        started.append(copy)

    def arrived(buffer, recv_sem):
        pltpu.make_async_remote_copy(
            src_ref=buffer, dst_ref=buffer, send_sem=recv_sem, recv_sem=recv_sem,
            device_id=sibling, device_id_type=MESH,
        ).wait_recv()

    def origin(way, step, d):
        zz = (z - step + NZ) % NZ if way == 0 else (z + step) % NZ
        return ((y + NY - d) % NY) * NZ + zz

    def pass_on(way, step, d):
        ref = src.at[origin(way, step, d)]
        send(ref, ref, gz_s.at[way, step, d], gz_r.at[way, step, d], at_z(1 if way == 0 else -1))

    for d in (1, 3, 2):
        send(src.at[row], src.at[row], gy_s.at[d], gy_r.at[d], at_y(d))
    for way in (0, 1):
        pass_on(way, 0, 0)

    lane = lax.broadcasted_iota(I32, (1, BS), 1)
    place = jnp.where(lane < cnt[0, 0], brow[...] * 32 + bcol[...], -1)
    place = jnp.broadcast_to(place, (BS, BS)).T
    slot = lax.broadcasted_iota(I32, (BS, BS), 0)
    spot = lax.broadcasted_iota(I32, (BS, BS), 1)
    for q in range(4):
        hit = jnp.where(place == spot + q * BS, slot - CAP, 0)
        inv_v[q : q + 1, :] = jnp.sum(hit, axis=0, keepdims=True) + CAP
    inv_v[4:8, :] = jnp.zeros((4, BS), I32)
    inv_copy = pltpu.make_async_copy(inv_v, inv_s, inv_sem)
    inv_copy.start()
    blocks[CAP] = jnp.zeros((BS, BS), BF)
    turned[CAP] = jnp.zeros((BS, BS), BF)

    for d in (1, 3, 2):
        arrived(src.at[origin(0, 0, d)], gy_r.at[d])
        for way in (0, 1):
            pass_on(way, 0, d)

    def lookup(r, c):
        return inv_s[r // 4, (r % 4) * 32 + c]

    def strip(z_at):
        return jnp.concatenate([src[yy * NZ + z_at] for yy in range(NY)], axis=0)

    def tile_rows(rows, z_at):
        return jnp.concatenate(
            [
                jnp.concatenate([blocks[lookup(r, yy * NZ + z_at)] for yy in range(NY)], axis=1)
                for r in rows
            ],
            axis=0,
        )

    def add_strip(z_at, first):
        def some(g, carry):
            out = jnp.dot(
                tile_rows([g * 4 + i for i in range(4)], z_at), strip(z_at),
                preferred_element_type=F32,
            ).reshape(4, BS, F)
            if first:
                acc[pl.ds(g * 4, 4)] = out
            else:
                acc[pl.ds(g * 4, 4)] += out
            return carry

        lax.fori_loop(0, 4, some, 0)

    def turn(first, last):
        def one(k, carry):
            turned[k] = blocks[k].T
            return carry

        lax.fori_loop(first, last, one, 0)

    adj_copy.wait()
    inv_copy.wait()
    add_strip(z, True)

    for step in range(4):
        for d in GATHER_ORDER:
            for way in (0, 1):
                if gather_has(way, step, d):
                    arrived(src.at[origin(way, step + 1, d)], gz_r.at[way, step, d])
                    if gather_has(way, step + 1, d):
                        pass_on(way, step + 1, d)
        if step < 3:
            add_strip((z + NZ - step - 1) % NZ, False)
            add_strip((z + step + 1) % NZ, False)
            turn(step * CAP // 3, (step + 1) * CAP // 3)

    far = (z + 4) % NZ
    for ours in (False, True):
        which = core if ours else 1 - core
        for g in (0, 1):
            ks = range(g * 4, g * 4 + 4)
            rows = [chip_at(k) * 2 + which for k in ks]
            out = jnp.dot(tile_rows(rows, far), strip(far), preferred_element_type=F32)
            for i, k in enumerate(ks):
                total = acc[rows[i]] + out[i * BS : (i + 1) * BS]
                if ours:
                    acc[rows[i]] = total
                else:
                    pair_out[k] = total.astype(BF)
            if not ours:
                group = pl.ds(g * 4, 4)
                send(pair_out.at[group], pair_in.at[group], pair_s.at[g], pair_r.at[g], sibling)
    for g in (0, 1):
        group = pl.ds(g * 4, 4)
        arrived(pair_in.at[group], pair_r.at[g])
        for k in range(g * 4, g * 4 + 4):
            total = acc[chip_at(k) * 2 + core] + pair_in[k].astype(F32)
            if k < CHIPS - 1:
                chip_out[k] = total.astype(BF)
                send(chip_out.at[k], chip_in.at[k], chip_s.at[k], chip_r.at[k], at_chip(k))
    for k in reversed(range(CHIPS - 1)):
        arrived(chip_in.at[k], chip_r.at[k])
        total = total + chip_in[k].astype(F32)

    row_scale = down_rows(scale_of(deg[pl.ds(row * (CHIPS * 2) + col, 1), :]), F)
    propagated = (total * row_scale).astype(BF)
    pre = jnp.dot(propagated, weight[...], preferred_element_type=F32)
    square = pre * pre
    tanh = jnp.tanh(GELU_A * (pre + GELU_B * (square * pre)))
    cdf = 0.5 * (1.0 + tanh)
    slope = cdf + 0.5 * pre * (1.0 - tanh * tanh) * (GELU_A * (1.0 + 3.0 * GELU_B * square))
    pre_grad = (cot[...].astype(F32) * slope).astype(BF)
    back = lax.dot_general(
        pre_grad, weight[...], (((1,), (1,)), ((), ())), preferred_element_type=F32
    )
    grads[col] = (back * row_scale).astype(BF)

    mine = grads.at[col]
    for k in range(CHIPS - 1):
        send(mine, mine, ag_s.at[k], ag_r.at[k], at_chip(k))
    send(mine, mine, fw_s.at[CHIPS - 1], fw_r.at[CHIPS - 1], sibling)

    act_out[...] = (pre * cdf).astype(BF)
    w_local = lax.dot_general(
        propagated, pre_grad, (((0,), (0,)), ((), ())), preferred_element_type=F32
    )
    part[0] = w_local[0:BS]
    part[1] = w_local[BS:F]
    w_half_out[...] = part[1 - core].astype(BF)
    send(w_half_out, w_half_in, wh_s, wh_r, sibling)

    for k in reversed(range(CHIPS - 1)):
        ref = grads.at[chip_from(k) * 2 + core]
        arrived(ref, ag_r.at[k])
        send(ref, ref, fw_s.at[k], fw_r.at[k], sibling)

    arrived(w_half_in, wh_r)
    half = part[core] + w_half_in[...].astype(F32)
    for c in range(CHIPS):
        w_piece_out[c] = half[c * 16 : (c + 1) * 16].astype(BF)
    for k in range(CHIPS - 1):
        send(w_piece_out.at[chip_at(k)], w_piece_in.at[k], wp_s.at[k], wp_r.at[k], at_chip(k))

    for k in reversed(range(CHIPS)):
        arrived(grads.at[chip_from(k) * 2 + 1 - core], fw_r.at[k])

    def back_strip(z_at, target):
        lhs = jnp.concatenate(
            [
                jnp.concatenate(
                    [turned[lookup(r, ((y + d) % NY) * NZ + z_at)] for r in range(16)], axis=1
                )
                for d in range(NY)
            ],
            axis=0,
        )
        out = jnp.dot(lhs, grads[...].reshape(16 * BS, F), preferred_element_type=F32)
        part[pl.ds(target * NY, NY)] = out.reshape(NY, BS, F)

    def w_step(step):
        if step == 0:
            total = w_piece_out[chip].astype(F32)
            for k in range(CHIPS - 1):
                arrived(w_piece_in.at[k], wp_r.at[k])
                total = total + w_piece_in[k].astype(F32)
            w_z[z] = total.astype(BF)
            for k in range(1, NZ):
                send(w_z.at[z], w_z.at[z], wz_s.at[k], wz_r.at[k], at_z(k))
        if step == 1:
            for k in range(1, NZ):
                arrived(w_z.at[(z + NZ - k) % NZ], wz_r.at[k])
            total = w_z[0].astype(F32)
            for k in range(1, NZ):
                total = total + w_z[k].astype(F32)
            w_y[y] = total.astype(BF)
            for d in range(1, NY):
                send(w_y.at[y], w_y.at[y], wy_s.at[d], wy_r.at[d], at_y(d))
        if step == 2:
            for d in range(1, NY):
                arrived(w_y.at[(y + NY - d) % NY], wy_r.at[d])
            total = w_y[0].astype(F32)
            for d in range(1, NY):
                total = total + w_y[d].astype(F32)
            w_all[chip] = total.astype(BF)
            for k in range(CHIPS - 1):
                send(w_all.at[chip], w_all.at[chip], wa_s.at[k], wa_r.at[k], at_chip(k))
        if step == 3:
            for k in range(CHIPS - 1):
                arrived(w_all.at[chip_from(k)], wa_r.at[k])
            send(w_all, w_other, wo_s, wo_r, sibling)

    back_strip((z + 4) % NZ, 0)
    for step in range(4):
        for d in SCATTER_ORDER:
            for way in (0, 1):
                if not scatter_has(way, step, d):
                    continue
                value = part[(way if step else 0) * NY + d]
                if step and scatter_has(way, step - 1, d):
                    arrived(ring_in.at[way, step - 1, d], rz_r.at[way, step - 1, d])
                    value = value + ring_in[way, step - 1, d].astype(F32)
                ring_out[way, step, d] = value.astype(BF)
                send(
                    ring_out.at[way, step, d], ring_in.at[way, step, d],
                    rz_s.at[way, step, d], rz_r.at[way, step, d], at_z(1 if way == 0 else -1),
                )
        if step < 3:
            back_strip((z + 3 - step) % NZ, 0)
            back_strip((z + NZ - 3 + step) % NZ, 1)
        else:
            back_strip(z, 0)
        w_step(step)

    for d in SCATTER_ORDER:
        value = part[d]
        for way in (0, 1):
            arrived(ring_in.at[way, 3, d], rz_r.at[way, 3, d])
            value = value + ring_in[way, 3, d].astype(F32)
        if d:
            last_out[d] = value.astype(BF)
            send(last_out.at[d], last_in.at[d], ry_s.at[d], ry_r.at[d], at_y(d))

    arrived(w_other, wo_r)
    wg_out[pl.ds(pl.multiple_of(core * BS, BS), BS), :] = w_all[...].astype(F32).reshape(BS, F)
    wg_out[pl.ds(pl.multiple_of((1 - core) * BS, BS), BS), :] = (
        w_other[...].astype(F32).reshape(BS, F)
    )

    for d in (1, 3, 2):
        arrived(last_in.at[d], ry_r.at[d])
        value = value + last_in[d].astype(F32)
    fg_out[...] = (value * own_scale).astype(BF)

    for copy in started:
        copy.wait_send()


def per_device(
    features, weight, cotangent, degrees, adj_blocks, block_rows, block_cols, block_count
):
    vmem = pl.BlockSpec(memory_space=pltpu.VMEM)
    dma = pltpu.SemaphoreType.DMA
    block = (BS, F)
    scratch = [
        pltpu.VMEM((CAP + 1, BS, BS), BF),
        pltpu.VMEM((CAP + 1, BS, BS), BF),
        pltpu.VMEM((NY * NZ,) + block, BF),
        pltpu.VMEM((CHIPS * 2,) + block, F32),
        pltpu.VMEM((8, BS), I32),
        pltpu.SMEM((8, BS), I32),
        pltpu.VMEM((CHIPS,) + block, BF),
        pltpu.VMEM((CHIPS,) + block, BF),
        pltpu.VMEM((CHIPS,) + block, BF),
        pltpu.VMEM((CHIPS,) + block, BF),
        pltpu.VMEM((CHIPS * 2,) + block, BF),
        pltpu.VMEM((2 * NY,) + block, F32),
        pltpu.VMEM((2, 4, NY) + block, BF),
        pltpu.VMEM((2, 4, NY) + block, BF),
        pltpu.VMEM((NY,) + block, BF),
        pltpu.VMEM((NY,) + block, BF),
        pltpu.VMEM(block, BF),
        pltpu.VMEM(block, BF),
        pltpu.VMEM((CHIPS, 16, F), BF),
        pltpu.VMEM((CHIPS, 16, F), BF),
        pltpu.VMEM((NZ, 16, F), BF),
        pltpu.VMEM((NY, 16, F), BF),
        pltpu.VMEM((CHIPS, 16, F), BF),
        pltpu.VMEM((CHIPS, 16, F), BF),
    ]
    sems = [dma, dma]
    for shape in (
        (NY,), (2, 4, NY), (2,), (CHIPS,), (CHIPS,), (CHIPS,), (2, 4, NY), (NY,),
        None, (CHIPS,), (NZ,), (NY,), (CHIPS,), None,
    ):
        sems += [dma if shape is None else dma(shape)] * 2
    return pl.pallas_call(
        kernel,
        out_shape=(
            jax.ShapeDtypeStruct(block, BF),
            jax.ShapeDtypeStruct(block, BF),
            jax.ShapeDtypeStruct((F, F), F32),
        ),
        in_specs=[vmem, vmem, vmem, vmem, pl.BlockSpec(memory_space=pl.ANY), vmem, vmem]
        + [pl.BlockSpec(memory_space=pltpu.SMEM)],
        out_specs=(vmem, vmem, vmem),
        scratch_shapes=scratch + sems,
        compiler_params=pltpu.CompilerParams(
            collective_id=0, has_side_effects=True, vmem_limit_bytes=48 * 1024 * 1024
        ),
        cost_estimate=pl.CostEstimate(
            flops=8 * 2048 * 4096 * 256 // 2, bytes_accessed=5 * 1024 * 1024, transcendentals=32768
        ),
        name="layer",
    )(
        features,
        weight,
        cotangent,
        degrees.reshape(-1, BS),
        adj_blocks.reshape(CAP, BS, BS),
        block_rows.reshape(1, CAP),
        block_cols.reshape(1, CAP),
        block_count,
    )


def solution(mesh):
    in_specs = (
        P(("col", "row"), None),
        P(),
        P(("row", "col"), None),
        P(),
        P("row", "col", None, None, None),
        P("row", "col", None),
        P("row", "col", None),
        P("row", "col"),
    )
    out_specs = (P(("row", "col"), None), P(("col", "row"), None), P())
    return jax.shard_map(
        per_device, mesh=mesh, in_specs=in_specs, out_specs=out_specs, check_vma=False
    )
```

time: 861 us -> 110 us (0.13)
  waiting for transfers between devices: 680 us -> 0 us
  Pallas kernels: 0 us -> 99.2 us
  other arithmetic: 91.2 us -> 0 us
  local copies, waits for them, and re-layouts: 45.2 us -> 8.98 us
  matrix products: 27 us -> 0 us
  between operations: 13.8 us -> 1.3 us
    reduce_scatter x2 -> x0, waiting for transfers between devices: 283 us -> none  [the longest x1 221 us: per_device(): lax.psum_scatter(back_term.astype(jnp.bfloat16), 'row', scatter_dimension...]
    psum x1 -> x0, waiting for transfers between devices: 272 us -> none  [per_device(): weight_grad = lax.psum(local_wgrad, ('row', 'col'))]
    all_gather x2 -> x0, waiting for transfers between devices: 125 us -> none  [the longest x1 92 us: per_device(): col_source = lax.all_gather(scaled, 'row', axis=0, tiled=True)]
    pallas_call x0 -> x1, Pallas kernels: none -> 99.2 us  [per_device(): pl.pallas_call(kernel, out_shape=(jax.ShapeDtypeStruct(block, BF), jax.Sh...]
    scatter-add x16 -> x0, other arithmetic: 69.1 us -> none  [add_group(): return totals.at[dest].add(result, mode='drop')]
    gather x16 -> x0, local copies, waits for them, and re-layouts: 32.3 us -> none  [add_group(): picked = pieces[lax.dynamic_slice_in_dim(slot_index, offset, group_size, 0)]]
    dot_general x19 -> x0, matrix products: 27 us -> none  [the longest x16 23.5 us: add_group(): jnp.einsum(pattern, slab, picked, preferred_element_type=jnp.float32)]
    select_n x17 -> x0, other arithmetic: 12.4 us -> none  [the longest x16 11.6 us: add_group(): picked = pieces[lax.dynamic_slice_in_dim(slot_index, offset, group_size, 0)]]
  transfers between devices with their start and end apart: 5 -> 0, of which waited for: 5 -> 0; matrix products, arithmetic and copies ran while one was open for 1% -> 0% of each run, Pallas kernels for 0% -> 0%
where the time goes in v1:
time: 110 us; the launch traced here: 109 us
  Pallas kernels  99.2 us (90%)
  local copies, waits for them, and re-layouts  8.98 us (8%)
  between operations  1.3 us (1%)
    pallas_call x1, Pallas kernels, per_device(): pl.pallas_call(kernel, out_shape=(jax.ShapeDtypeStruct(block, BF), jax.Sh...  99.2 us
    unnamed x17, local copies, waits for them, and re-layouts  8.98 us

profile of v1, /device:TPU:1, one launch (start us, length us, event | category | flops | bytes accessed | tf_op | source)
XLA Modules:
  0.0 109.5 jit_solution(7525746830665772580)
XLA Ops:
  1.3 0.0 copy-start
  1.3 2.2 %copy-done = bf16[1,1,128,128,128]{4,3,2,1,0:T(8,128)(2,1)S(1)} copy-done((bf16[1,1,128,128,128]{4,3,2,1,0:T(8,128)(2,1)S(1)}, bf16[1,1,128,128,128]{4,3,2,1,0:T(8,128)(2,1)}, u32[]{:S(2)}) %copy-start) | copy-done | bytes 4194328
  3.5 0.0 copy-start.1
  3.5 0.9 copy-done.1
  4.4 0.0 copy-start.2
  4.4 0.9 copy-done.2
  5.3 0.0 copy-start.3
  5.3 0.8 copy-done.3
  6.2 0.0 copy-start.4
  6.2 0.8 copy-done.4
  7.0 0.0 copy-start.5
  7.0 0.7 copy-done.5
  7.7 0.0 copy-start.6
  7.7 0.7 copy-done.6
  8.3 99.2 %layer.1 = (bf16[128,256]{1,0:T(8,128)(2,1)S(1)}, bf16[128,256]{1,0:T(8,128)(2,1)S(1)}, f32[256,256]{1,0:T(8,128)S(1)}) custom-call(bf16[128,256]{1,0:T(8,128)(2,1)S(1)} %copy-done.3, bf16[256,256]{1,0:T(8,128)(2,1)S(1)} %copy-done.2, bf16[128,256]{1,0:T(8,128)(2,1)S(1)} %copy-done.4, s32[512,128]{1,0:T(8,128)S(1)} %bitcast.5, ...), custom_call_target="tpu_custom_call" | custom-call | flops 8589934592 | bytes 5242880 | tf_op jit(solution)/shard_map/layer/pallas_call | solution.py:394
  107.5 0.6 copy.15
  108.1 0.6 copy.16
  108.8 0.7 copy.17
Async XLA Ops:
  1.3 2.2 %copy-start = (bf16[1,1,128,128,128]{4,3,2,1,0:T(8,128)(2,1)S(1)}, bf16[1,1,128,128,128]{4,3,2,1,0:T(8,128)(2,1)}, u32[]{:S(2)}) copy-start(bf16[1,1,128,128,128]{4,3,2,1,0:T(8,128)(2,1)} %param.12) | copy-start | bytes 12582916
  3.5 0.9 copy-start.1
  4.4 0.9 copy-start.2
  5.3 0.8 copy-start.3
  6.2 0.8 copy-start.4
  7.0 0.7 copy-start.5
  7.7 0.7 copy-start.6

commit v2 on v1

--- a/solution.py
+++ b/solution.py
@@ -19,8 +19,35 @@
 GELU_A = math.sqrt(2.0 / math.pi)
 GELU_B = 0.044715
 
-GATHER_ORDER = (0, 1, 3, 2)
-SCATTER_ORDER = (2, 1, 3, 0)
+TALL = 96
+G_PIECES, S_PIECES = 1, 1
+G_ROWS, S_ROWS = TALL // G_PIECES, TALL // S_PIECES
+GATHER = (
+    ("z", 0, 0, 0, 0), ("z", 0, 1, 0, 0), ("b", 0, 0), ("b", 1, 0), ("y", 0, 1), ("y", 0, 3),
+    ("z", 0, 0, 1, 0), ("z", 0, 1, 1, 0), ("b", 0, 1), ("b", 1, 1), ("z", 0, 0, 0, 1), ("y", 0, 2),
+    ("z", 0, 1, 0, 1), ("q", 0, 1), ("q", 0, 3), ("q", 0, 2), ("c", 0), ("z", 0, 0, 0, 3),
+    ("z", 0, 1, 0, 3), ("q", 1, 1), ("q", 1, 3), ("z", 0, 0, 2, 0), ("q", 1, 2), ("z", 0, 1, 2, 0),
+    ("b", 0, 2), ("b", 1, 2), ("q", 5, 1), ("q", 5, 3), ("z", 0, 0, 1, 1), ("q", 5, 2),
+    ("z", 0, 1, 0, 2), ("c", 5), ("z", 0, 0, 0, 2), ("q", 2, 1), ("c", 1), ("q", 2, 3),
+    ("z", 0, 1, 1, 1), ("q", 2, 2), ("z", 0, 0, 1, 3), ("z", 0, 1, 1, 3), ("q", 6, 1), ("q", 6, 3),
+    ("q", 6, 2), ("z", 0, 0, 3, 0), ("z", 0, 1, 1, 2), ("c", 6), ("b", 0, 3), ("q", 3, 1),
+    ("q", 3, 3), ("q", 3, 2), ("z", 0, 0, 2, 1), ("z", 0, 1, 2, 1), ("q", 7, 1), ("q", 7, 3),
+    ("z", 0, 0, 1, 2), ("q", 7, 2), ("c", 2), ("z", 0, 1, 2, 3), ("z", 0, 0, 2, 3),
+    ("z", 0, 1, 2, 2), ("c", 7), ("z", 0, 0, 3, 1), ("q", 4, 1), ("q", 4, 3), ("q", 4, 2),
+    ("z", 0, 0, 2, 2), ("c", 3), ("z", 0, 1, 3, 3), ("z", 0, 1, 3, 2),
+)
+SCATTER = (
+    ("c", 4), ("z", 0, 0, 0, 2), ("z", 0, 1, 0, 1), ("z", 0, 1, 0, 3), ("z", 0, 0, 0, 0), ("q", 4),
+    ("c", 3), ("z", 0, 0, 1, 1), ("z", 0, 0, 1, 3), ("q", 3), ("c", 7), ("z", 0, 1, 1, 2),
+    ("z", 0, 1, 1, 0), ("q", 7), ("z", 0, 0, 1, 2), ("z", 0, 1, 1, 1), ("c", 2), ("q", 2), ("w", 0),
+    ("z", 0, 1, 1, 3), ("z", 0, 0, 1, 0), ("c", 6), ("b", 0, 0), ("z", 0, 0, 2, 1), ("q", 6),
+    ("z", 0, 1, 2, 2), ("c", 1), ("z", 0, 0, 2, 3), ("q", 1), ("z", 0, 1, 2, 0), ("c", 5),
+    ("z", 0, 0, 2, 2), ("w", 1), ("q", 5), ("b", 1, 1), ("z", 0, 1, 2, 1), ("z", 0, 0, 2, 0),
+    ("c", 0), ("b", 0, 1), ("z", 0, 1, 2, 3), ("q", 0), ("z", 0, 0, 3, 1), ("z", 0, 1, 3, 2),
+    ("z", 0, 0, 3, 3), ("z", 0, 1, 3, 0), ("w", 2), ("b", 1, 2), ("z", 0, 0, 3, 2),
+    ("z", 0, 1, 3, 1), ("z", 0, 0, 3, 0), ("b", 0, 2), ("z", 0, 1, 3, 3), ("w", 3), ("b", 1, 3),
+    ("y", 0, 2), ("y", 0, 1), ("b", 0, 3), ("y", 0, 3), ("s",), ("t", 0),
+)
 CHIP_ORDER = ((1, 2), (1, 1), (1, 3), (1, 0), (0, 2), (0, 1), (0, 3), (0, 0))
 
 
@@ -34,24 +61,39 @@
     return jnp.concatenate([square] * (width // BS), axis=1) if width > BS else square
 
 
+def short_has(way, step):
+    return step < 3 or (step == 3 and way == 0)
+
+
+def short_at(way, step):
+    return 1 + step + 4 * way
+
+
 def gather_has(way, step, d):
     return step < 3 or (step == 3 and (d in (0, 1)) == (way == 0))
 
 
+def short_ring_has(way, step):
+    return step > 0 or way == 0
+
+
 def scatter_has(way, step, d):
     return step > 0 or (d in (2, 0)) == (way == 0)
 
 
 def kernel(
-    feat, weight, cot, deg, adj, brow, bcol, cnt,
+    feat_h, weight_h, cot_h, deg_h, adj, brow_h, bcol_h, cnt_h,
     act_out, fg_out, wg_out,
+    feat, weight, cot, deg, brow, bcol, cnt,
     blocks, turned, src, acc, inv_v, inv_s,
     pair_out, pair_in, chip_out, chip_in, grads,
     part, ring_out, ring_in, last_out, last_in,
     w_half_out, w_half_in, w_piece_out, w_piece_in, w_z, w_y, w_all, w_other,
-    adj_sem, inv_sem, gy_s, gy_r, gz_s, gz_r, pair_s, pair_r, chip_s, chip_r,
+    short_out, short_in, short_ring_out, short_ring_in,
+    in_sem, adj_sem, inv_sem, gy_s, gy_r, gz_s, gz_r, pair_s, pair_r, chip_s, chip_r,
     ag_s, ag_r, fw_s, fw_r, rz_s, rz_r, ry_s, ry_r,
     wh_s, wh_r, wp_s, wp_r, wz_s, wz_r, wy_s, wy_r, wa_s, wa_r, wo_s, wo_r,
+    hz_s, hz_r, hy_s, hy_r, kz_s, kz_r, ky_s, ky_r,
 ):
     row = lax.axis_index("row")
     col = lax.axis_index("col")
@@ -78,6 +120,17 @@
 
     sibling = (row, chip * 2 + 1 - core)
 
+    loads = [
+        pltpu.make_async_copy(source, target, in_sem.at[i])
+        for i, (source, target) in enumerate(
+            (
+                (deg_h, deg), (feat_h, feat), (brow_h, brow), (bcol_h, bcol),
+                (cnt_h, cnt), (weight_h, weight), (cot_h, cot),
+            )
+        )
+    ]
+    for load in loads:
+        load.start()
     adj_copy = pltpu.make_async_copy(adj, blocks.at[pl.ds(0, CAP)], adj_sem)
     adj_copy.start()
 
@@ -87,40 +140,13 @@
     for partner in partners:
         pl.semaphore_signal(barrier, inc=1, device_id=partner, device_id_type=MESH)
 
+    for load in loads[:2]:
+        load.wait()
     own_scale = down_rows(scale_of(deg[pl.ds(col * (NY * NZ) + row, 1), :]), F)
     src[row] = (feat[...].astype(F32) * own_scale).astype(BF)
 
-    pl.semaphore_wait(barrier, len(partners))
-
-    started = []
-
-    def send(source, target, send_sem, recv_sem, device):
-        copy = pltpu.make_async_remote_copy(
-            src_ref=source, dst_ref=target, send_sem=send_sem, recv_sem=recv_sem,
-            device_id=device, device_id_type=MESH,
-        )
-        copy.start()
-        started.append(copy)
-
-    def arrived(buffer, recv_sem):
-        pltpu.make_async_remote_copy(
-            src_ref=buffer, dst_ref=buffer, send_sem=recv_sem, recv_sem=recv_sem,
-            device_id=sibling, device_id_type=MESH,
-        ).wait_recv()
-
-    def origin(way, step, d):
-        zz = (z - step + NZ) % NZ if way == 0 else (z + step) % NZ
-        return ((y + NY - d) % NY) * NZ + zz
-
-    def pass_on(way, step, d):
-        ref = src.at[origin(way, step, d)]
-        send(ref, ref, gz_s.at[way, step, d], gz_r.at[way, step, d], at_z(1 if way == 0 else -1))
-
-    for d in (1, 3, 2):
-        send(src.at[row], src.at[row], gy_s.at[d], gy_r.at[d], at_y(d))
-    for way in (0, 1):
-        pass_on(way, 0, 0)
-
+    for load in loads[2:5]:
+        load.wait()
     lane = lax.broadcasted_iota(I32, (1, BS), 1)
     place = jnp.where(lane < cnt[0, 0], brow[...] * 32 + bcol[...], -1)
     place = jnp.broadcast_to(place, (BS, BS)).T
@@ -135,10 +161,66 @@
     blocks[CAP] = jnp.zeros((BS, BS), BF)
     turned[CAP] = jnp.zeros((BS, BS), BF)
 
-    for d in (1, 3, 2):
-        arrived(src.at[origin(0, 0, d)], gy_r.at[d])
+    def turn(first, last):
+        def one(k, carry):
+            turned[k] = blocks[k].T
+            return carry
+
+        lax.fori_loop(first, last, one, 0)
+
+    adj_copy.wait()
+    turn(0, CAP // 2)
+    pl.semaphore_wait(barrier, len(partners))
+
+    started = []
+
+    def send(source, target, send_sem, recv_sem, device):
+        copy = pltpu.make_async_remote_copy(
+            src_ref=source, dst_ref=target, send_sem=send_sem, recv_sem=recv_sem,
+            device_id=device, device_id_type=MESH,
+        )
+        copy.start()
+        started.append(copy)
+
+    def arrived(buffer, recv_sem):
+        pltpu.make_async_remote_copy(
+            src_ref=buffer, dst_ref=buffer, send_sem=recv_sem, recv_sem=recv_sem,
+            device_id=sibling, device_id_type=MESH,
+        ).wait_recv()
+
+    def origin(way, step, d):
+        zz = (z - step + NZ) % NZ if way == 0 else (z + step) % NZ
+        return ((y + NY - d) % NY) * NZ + zz
+
+    def tall(r, c):
+        return src.at[r, pl.ds(c * G_ROWS, G_ROWS)]
+
+    def short(r):
+        return src.at[r, pl.ds(TALL, BS - TALL)]
+
+    def pass_on(c, way, step, d):
+        ref = tall(origin(way, step, d), c)
+        i = d * G_PIECES + c
+        send(ref, ref, gz_s.at[way, step, i], gz_r.at[way, step, i], at_z(1 if way == 0 else -1))
+
+    def short_pass_on(way, step):
+        ref = short(origin(way, step, 0))
+        send(ref, ref, hz_s.at[way, step], hz_r.at[way, step], at_z(1 if way == 0 else -1))
+
+    def short_spread(i, r):
+        for d in (2, 1, 3):
+            send(short(r), short(r), hy_s.at[i, d], hy_r.at[i, d], at_y(d))
+
+    for c in range(G_PIECES):
         for way in (0, 1):
-            pass_on(way, 0, d)
+            pass_on(c, way, 0, 0)
+    for c in range(G_PIECES):
+        for d in (1, 3, 2):
+            i = d * G_PIECES + c
+            send(tall(row, c), tall(row, c), gy_s.at[i], gy_r.at[i], at_y(d))
+    for way in (0, 1):
+        short_pass_on(way, 0)
+    short_spread(0, row)
 
     def lookup(r, c):
         return inv_s[r // 4, (r % 4) * 32 + c]
@@ -169,28 +251,38 @@
 
         lax.fori_loop(0, 4, some, 0)
 
-    def turn(first, last):
-        def one(k, carry):
-            turned[k] = blocks[k].T
-            return carry
-
-        lax.fori_loop(first, last, one, 0)
-
-    adj_copy.wait()
+    def strip_way(i):
+        return (0, i) if i <= 4 else (1, i - 4)
+
+    def strip_z(i):
+        way, step = strip_way(i)
+        return (z - step + NZ) % NZ if way == 0 else (z + step) % NZ
+
+    turn(CAP // 2, CAP)
     inv_copy.wait()
-    add_strip(z, True)
-
-    for step in range(4):
-        for d in GATHER_ORDER:
+    for what, *of in GATHER:
+        if what == "y":
+            c, d = of
+            arrived(tall(origin(0, 0, d), c), gy_r.at[d * G_PIECES + c])
             for way in (0, 1):
-                if gather_has(way, step, d):
-                    arrived(src.at[origin(way, step + 1, d)], gz_r.at[way, step, d])
-                    if gather_has(way, step + 1, d):
-                        pass_on(way, step + 1, d)
-        if step < 3:
-            add_strip((z + NZ - step - 1) % NZ, False)
-            add_strip((z + step + 1) % NZ, False)
-            turn(step * CAP // 3, (step + 1) * CAP // 3)
+                pass_on(c, way, 0, d)
+        elif what == "z":
+            c, way, step, d = of
+            arrived(tall(origin(way, step + 1, d), c), gz_r.at[way, step, d * G_PIECES + c])
+            if gather_has(way, step + 1, d):
+                pass_on(c, way, step + 1, d)
+        elif what == "b":
+            way, step = of
+            r = origin(way, step + 1, 0)
+            arrived(short(r), hz_r.at[way, step])
+            if short_has(way, step + 1):
+                short_pass_on(way, step + 1)
+            short_spread(short_at(way, step), r)
+        elif what == "q":
+            i, d = of
+            arrived(short(origin(*strip_way(i), d)), hy_r.at[i, d])
+        else:
+            add_strip(strip_z(of[0]), of[0] == 0)
 
     far = (z + 4) % NZ
     for ours in (False, True):
@@ -220,6 +312,8 @@
         arrived(chip_in.at[k], chip_r.at[k])
         total = total + chip_in[k].astype(F32)
 
+    for load in loads[5:]:
+        load.wait()
     row_scale = down_rows(scale_of(deg[pl.ds(row * (CHIPS * 2) + col, 1), :]), F)
     propagated = (total * row_scale).astype(BF)
     pre = jnp.dot(propagated, weight[...], preferred_element_type=F32)
@@ -262,7 +356,9 @@
     for k in reversed(range(CHIPS)):
         arrived(grads.at[chip_from(k) * 2 + 1 - core], fw_r.at[k])
 
-    def back_strip(z_at, target):
+    def back_strip(i):
+        way, step = strip_way(i)
+        z_at = (z + step) % NZ if way == 0 else (z + NZ - step) % NZ
         lhs = jnp.concatenate(
             [
                 jnp.concatenate(
@@ -273,7 +369,7 @@
             axis=0,
         )
         out = jnp.dot(lhs, grads[...].reshape(16 * BS, F), preferred_element_type=F32)
-        part[pl.ds(target * NY, NY)] = out.reshape(NY, BS, F)
+        part[pl.ds(i * NY, NY)] = out.reshape(NY, BS, F)
 
     def w_step(step):
         if step == 0:
@@ -307,47 +403,79 @@
                 arrived(w_all.at[chip_from(k)], wa_r.at[k])
             send(w_all, w_other, wo_s, wo_r, sibling)
 
-    back_strip((z + 4) % NZ, 0)
-    for step in range(4):
-        for d in SCATTER_ORDER:
+    def short_total(i):
+        total = part[i * NY, TALL:BS]
+        for d in (1, 3, 2):
+            arrived(short_in.at[i, d], ky_r.at[i, d])
+            total = total + short_in[i, d].astype(F32)
+        return total
+
+    def rows_of(c):
+        return slice(c * S_ROWS, (c + 1) * S_ROWS)
+
+    def strip_at(way, step):
+        return 4 - step if way == 0 or step == 0 else 8 - step
+
+    for what, *of in SCATTER:
+        if what == "c":
+            back_strip(of[0])
+        elif what == "q":
+            i = of[0]
+            for d in (2, 1, 3):
+                short_out[i, d] = part[i * NY + d, TALL:BS].astype(BF)
+                send(short_out.at[i, d], short_in.at[i, d], ky_s.at[i, d], ky_r.at[i, d], at_y(d))
+        elif what == "z":
+            c, way, step, d = of
+            value = part[strip_at(way, step) * NY + d, rows_of(c)]
+            rows, i = pl.ds(c * S_ROWS, S_ROWS), d * S_PIECES + c
+            if step and scatter_has(way, step - 1, d):
+                arrived(ring_in.at[way, step - 1, d, rows], rz_r.at[way, step - 1, i])
+                value = value + ring_in[way, step - 1, d, rows_of(c)].astype(F32)
+            ring_out[way, step, d, rows_of(c)] = value.astype(BF)
+            send(
+                ring_out.at[way, step, d, rows], ring_in.at[way, step, d, rows],
+                rz_s.at[way, step, i], rz_r.at[way, step, i], at_z(1 if way == 0 else -1),
+            )
+        elif what == "b":
+            way, step = of
+            total = short_total(strip_at(way, step))
+            if step and short_ring_has(way, step - 1):
+                arrived(short_ring_in.at[way, step - 1], kz_r.at[way, step - 1])
+                total = total + short_ring_in[way, step - 1].astype(F32)
+            short_ring_out[way, step] = total.astype(BF)
+            send(
+                short_ring_out.at[way, step], short_ring_in.at[way, step],
+                kz_s.at[way, step], kz_r.at[way, step], at_z(1 if way == 0 else -1),
+            )
+        elif what == "w":
+            w_step(of[0])
+        elif what == "s":
+            total = short_total(0)
             for way in (0, 1):
-                if not scatter_has(way, step, d):
-                    continue
-                value = part[(way if step else 0) * NY + d]
-                if step and scatter_has(way, step - 1, d):
-                    arrived(ring_in.at[way, step - 1, d], rz_r.at[way, step - 1, d])
-                    value = value + ring_in[way, step - 1, d].astype(F32)
-                ring_out[way, step, d] = value.astype(BF)
-                send(
-                    ring_out.at[way, step, d], ring_in.at[way, step, d],
-                    rz_s.at[way, step, d], rz_r.at[way, step, d], at_z(1 if way == 0 else -1),
-                )
-        if step < 3:
-            back_strip((z + 3 - step) % NZ, 0)
-            back_strip((z + NZ - 3 + step) % NZ, 1)
+                arrived(short_ring_in.at[way, 3], kz_r.at[way, 3])
+                total = total + short_ring_in[way, 3].astype(F32)
+            fg_out[TALL:BS, :] = (total * own_scale[TALL:BS]).astype(BF)
         else:
-            back_strip(z, 0)
-        w_step(step)
-
-    for d in SCATTER_ORDER:
-        value = part[d]
-        for way in (0, 1):
-            arrived(ring_in.at[way, 3, d], rz_r.at[way, 3, d])
-            value = value + ring_in[way, 3, d].astype(F32)
-        if d:
-            last_out[d] = value.astype(BF)
-            send(last_out.at[d], last_in.at[d], ry_s.at[d], ry_r.at[d], at_y(d))
+            c, d = of[0], of[1] if what == "y" else 0
+            rows, i = pl.ds(c * S_ROWS, S_ROWS), d * S_PIECES + c
+            value = part[d, rows_of(c)]
+            for way in (0, 1):
+                arrived(ring_in.at[way, 3, d, rows], rz_r.at[way, 3, i])
+                value = value + ring_in[way, 3, d, rows_of(c)].astype(F32)
+            if what == "y":
+                last_out[d, rows_of(c)] = value.astype(BF)
+                send(last_out.at[d, rows], last_in.at[d, rows], ry_s.at[i], ry_r.at[i], at_y(d))
+                continue
+            for d in (1, 3, 2):
+                arrived(last_in.at[d, rows], ry_r.at[d * S_PIECES + c])
+                value = value + last_in[d, rows_of(c)].astype(F32)
+            fg_out[rows_of(c), :] = (value * own_scale[rows_of(c)]).astype(BF)
 
     arrived(w_other, wo_r)
     wg_out[pl.ds(pl.multiple_of(core * BS, BS), BS), :] = w_all[...].astype(F32).reshape(BS, F)
     wg_out[pl.ds(pl.multiple_of((1 - core) * BS, BS), BS), :] = (
         w_other[...].astype(F32).reshape(BS, F)
     )
-
-    for d in (1, 3, 2):
-        arrived(last_in.at[d], ry_r.at[d])
-        value = value + last_in[d].astype(F32)
-    fg_out[...] = (value * own_scale).astype(BF)
 
     for copy in started:
         copy.wait_send()
@@ -359,7 +487,15 @@
     vmem = pl.BlockSpec(memory_space=pltpu.VMEM)
     dma = pltpu.SemaphoreType.DMA
     block = (BS, F)
+    high, low = (TALL, F), (BS - TALL, F)
     scratch = [
+        pltpu.VMEM(block, BF),
+        pltpu.VMEM((F, F), BF),
+        pltpu.VMEM(block, BF),
+        pltpu.VMEM((512, BS), I32),
+        pltpu.VMEM((1, BS), I32),
+        pltpu.VMEM((1, BS), I32),
+        pltpu.SMEM((1, 1), I32),
         pltpu.VMEM((CAP + 1, BS, BS), BF),
         pltpu.VMEM((CAP + 1, BS, BS), BF),
         pltpu.VMEM((NY * NZ,) + block, BF),
@@ -371,11 +507,11 @@
         pltpu.VMEM((CHIPS,) + block, BF),
         pltpu.VMEM((CHIPS,) + block, BF),
         pltpu.VMEM((CHIPS * 2,) + block, BF),
-        pltpu.VMEM((2 * NY,) + block, F32),
-        pltpu.VMEM((2, 4, NY) + block, BF),
-        pltpu.VMEM((2, 4, NY) + block, BF),
-        pltpu.VMEM((NY,) + block, BF),
-        pltpu.VMEM((NY,) + block, BF),
+        pltpu.VMEM((NZ * NY,) + block, F32),
+        pltpu.VMEM((2, 4, NY) + high, BF),
+        pltpu.VMEM((2, 4, NY) + high, BF),
+        pltpu.VMEM((NY,) + high, BF),
+        pltpu.VMEM((NY,) + high, BF),
         pltpu.VMEM(block, BF),
         pltpu.VMEM(block, BF),
         pltpu.VMEM((CHIPS, 16, F), BF),
@@ -384,11 +520,17 @@
         pltpu.VMEM((NY, 16, F), BF),
         pltpu.VMEM((CHIPS, 16, F), BF),
         pltpu.VMEM((CHIPS, 16, F), BF),
+        pltpu.VMEM((NZ, NY) + low, BF),
+        pltpu.VMEM((NZ, NY) + low, BF),
+        pltpu.VMEM((2, 4) + low, BF),
+        pltpu.VMEM((2, 4) + low, BF),
     ]
-    sems = [dma, dma]
+    sems = [dma((7,)), dma, dma]
     for shape in (
-        (NY,), (2, 4, NY), (2,), (CHIPS,), (CHIPS,), (CHIPS,), (2, 4, NY), (NY,),
+        (NY * G_PIECES,), (2, 4, NY * G_PIECES), (2,), (CHIPS,), (CHIPS,), (CHIPS,),
+        (2, 4, NY * S_PIECES), (NY * S_PIECES,),
         None, (CHIPS,), (NZ,), (NY,), (CHIPS,), None,
+        (2, 4), (NZ, NY), (2, 4), (NZ, NY),
     ):
         sems += [dma if shape is None else dma(shape)] * 2
     return pl.pallas_call(
@@ -398,12 +540,11 @@
             jax.ShapeDtypeStruct(block, BF),
             jax.ShapeDtypeStruct((F, F), F32),
         ),
-        in_specs=[vmem, vmem, vmem, vmem, pl.BlockSpec(memory_space=pl.ANY), vmem, vmem]
-        + [pl.BlockSpec(memory_space=pltpu.SMEM)],
+        in_specs=[pl.BlockSpec(memory_space=pltpu.HBM)] * 8,
         out_specs=(vmem, vmem, vmem),
         scratch_shapes=scratch + sems,
         compiler_params=pltpu.CompilerParams(
-            collective_id=0, has_side_effects=True, vmem_limit_bytes=48 * 1024 * 1024
+            collective_id=0, has_side_effects=True, vmem_limit_bytes=58 * 1024 * 1024
         ),
         cost_estimate=pl.CostEstimate(
             flops=8 * 2048 * 4096 * 256 // 2, bytes_accessed=5 * 1024 * 1024, transcendentals=32768

time: 110 us -> 102 us (0.927)
  local copies, waits for them, and re-layouts: 8.98 us -> 4.61 us
  Pallas kernels: 99.2 us -> 95.7 us
    unnamed x17 -> x3, local copies, waits for them, and re-layouts: 8.98 us -> 4.61 us
    pallas_call x1, Pallas kernels: 99.2 us -> 95.7 us  [per_device(): pl.pallas_call(kernel, out_shape=(jax.ShapeDtypeStruct(block, BF), jax.Sh...]
where the time goes in v2:
time: 102 us
  Pallas kernels  95.7 us (94%)
  local copies, waits for them, and re-layouts  4.61 us (5%)
  between operations  1.29 us (1%)
    pallas_call x1, Pallas kernels, per_device(): pl.pallas_call(kernel, out_shape=(jax.ShapeDtypeStruct(block, BF), jax.Sh...  95.7 us
    unnamed x3, local copies, waits for them, and re-layouts  4.61 us

profile of v2, /device:TPU:1, one launch (start us, length us, event | category | flops | bytes accessed | tf_op | source)
XLA Modules:
  0.0 101.6 jit_solution(4747855897395595585)
XLA Ops:
  1.3 95.7 %layer.1 = (bf16[128,256]{1,0:T(8,128)(2,1)}, bf16[128,256]{1,0:T(8,128)(2,1)}, f32[256,256]{1,0:T(8,128)}) custom-call(bf16[128,256]{1,0:T(8,128)(2,1)} %feat_h.1, bf16[256,256]{1,0:T(8,128)(2,1)} %weight_h.1, bf16[128,256]{1,0:T(8,128)(2,1)} %cot_h.1, s32[512,128]{1,0:T(8,128)} %bitcast.5, bf16[128,128,128]{2,1,0:T(8,128)(2,1)} %bitcast.4, ...), custom_call_target="tpu_custom_call" | custom-call | flops 8589934592 | bytes 5242880 | tf_op jit(solution)/shard_map/layer/pallas_call | solution.py:536
  97.0 1.5 %copy.15 = bf16[128,256]{1,0:T(8,128)(2,1)} copy(bf16[128,256]{1,0:T(8,128)(2,1)} %get-tuple-element.6) | data formatting | bytes 131072
  98.4 1.5 %copy.16 = bf16[128,256]{1,0:T(8,128)(2,1)} copy(bf16[128,256]{1,0:T(8,128)(2,1)} %get-tuple-element.7) | data formatting | bytes 131072
  99.9 1.7 %copy.17 = f32[256,256]{1,0:T(8,128)} copy(f32[256,256]{1,0:T(8,128)} %get-tuple-element.8) | data formatting | bytes 524288

commit v3 on v2

--- a/solution.py
+++ b/solution.py
@@ -145,6 +145,58 @@
     own_scale = down_rows(scale_of(deg[pl.ds(col * (NY * NZ) + row, 1), :]), F)
     src[row] = (feat[...].astype(F32) * own_scale).astype(BF)
 
+    pl.semaphore_wait(barrier, len(partners))
+
+    started = []
+
+    def send(source, target, send_sem, recv_sem, device):
+        copy = pltpu.make_async_remote_copy(
+            src_ref=source, dst_ref=target, send_sem=send_sem, recv_sem=recv_sem,
+            device_id=device, device_id_type=MESH,
+        )
+        copy.start()
+        started.append(copy)
+
+    def arrived(buffer, recv_sem):
+        pltpu.make_async_remote_copy(
+            src_ref=buffer, dst_ref=buffer, send_sem=recv_sem, recv_sem=recv_sem,
+            device_id=sibling, device_id_type=MESH,
+        ).wait_recv()
+
+    def origin(way, step, d):
+        zz = (z - step + NZ) % NZ if way == 0 else (z + step) % NZ
+        return ((y + NY - d) % NY) * NZ + zz
+
+    def tall(r, c):
+        return src.at[r, pl.ds(c * G_ROWS, G_ROWS)]
+
+    def short(r):
+        return src.at[r, pl.ds(TALL, BS - TALL)]
+
+    def pass_on(c, way, step, d):
+        ref = tall(origin(way, step, d), c)
+        i = d * G_PIECES + c
+        send(ref, ref, gz_s.at[way, step, i], gz_r.at[way, step, i], at_z(1 if way == 0 else -1))
+
+    def short_pass_on(way, step):
+        ref = short(origin(way, step, 0))
+        send(ref, ref, hz_s.at[way, step], hz_r.at[way, step], at_z(1 if way == 0 else -1))
+
+    def short_spread(i, r):
+        for d in (2, 1, 3):
+            send(short(r), short(r), hy_s.at[i, d], hy_r.at[i, d], at_y(d))
+
+    for c in range(G_PIECES):
+        for way in (0, 1):
+            pass_on(c, way, 0, 0)
+    for c in range(G_PIECES):
+        for d in (1, 3, 2):
+            i = d * G_PIECES + c
+            send(tall(row, c), tall(row, c), gy_s.at[i], gy_r.at[i], at_y(d))
+    for way in (0, 1):
+        short_pass_on(way, 0)
+    short_spread(0, row)
+
     for load in loads[2:5]:
         load.wait()
     lane = lax.broadcasted_iota(I32, (1, BS), 1)
@@ -168,60 +220,6 @@
 
         lax.fori_loop(first, last, one, 0)
 
-    adj_copy.wait()
-    turn(0, CAP // 2)
-    pl.semaphore_wait(barrier, len(partners))
-
-    started = []
-
-    def send(source, target, send_sem, recv_sem, device):
-        copy = pltpu.make_async_remote_copy(
-            src_ref=source, dst_ref=target, send_sem=send_sem, recv_sem=recv_sem,
-            device_id=device, device_id_type=MESH,
-        )
-        copy.start()
-        started.append(copy)
-
-    def arrived(buffer, recv_sem):
-        pltpu.make_async_remote_copy(
-            src_ref=buffer, dst_ref=buffer, send_sem=recv_sem, recv_sem=recv_sem,
-            device_id=sibling, device_id_type=MESH,
-        ).wait_recv()
-
-    def origin(way, step, d):
-        zz = (z - step + NZ) % NZ if way == 0 else (z + step) % NZ
-        return ((y + NY - d) % NY) * NZ + zz
-
-    def tall(r, c):
-        return src.at[r, pl.ds(c * G_ROWS, G_ROWS)]
-
-    def short(r):
-        return src.at[r, pl.ds(TALL, BS - TALL)]
-
-    def pass_on(c, way, step, d):
-        ref = tall(origin(way, step, d), c)
-        i = d * G_PIECES + c
-        send(ref, ref, gz_s.at[way, step, i], gz_r.at[way, step, i], at_z(1 if way == 0 else -1))
-
-    def short_pass_on(way, step):
-        ref = short(origin(way, step, 0))
-        send(ref, ref, hz_s.at[way, step], hz_r.at[way, step], at_z(1 if way == 0 else -1))
-
-    def short_spread(i, r):
-        for d in (2, 1, 3):
-            send(short(r), short(r), hy_s.at[i, d], hy_r.at[i, d], at_y(d))
-
-    for c in range(G_PIECES):
-        for way in (0, 1):
-            pass_on(c, way, 0, 0)
-    for c in range(G_PIECES):
-        for d in (1, 3, 2):
-            i = d * G_PIECES + c
-            send(tall(row, c), tall(row, c), gy_s.at[i], gy_r.at[i], at_y(d))
-    for way in (0, 1):
-        short_pass_on(way, 0)
-    short_spread(0, row)
-
     def lookup(r, c):
         return inv_s[r // 4, (r % 4) * 32 + c]
 
@@ -258,7 +256,8 @@
         way, step = strip_way(i)
         return (z - step + NZ) % NZ if way == 0 else (z + step) % NZ
 
-    turn(CAP // 2, CAP)
+    adj_copy.wait()
+    turn(0, CAP)
     inv_copy.wait()
     for what, *of in GATHER:
         if what == "y":
@@ -536,9 +535,9 @@
     return pl.pallas_call(
         kernel,
         out_shape=(
-            jax.ShapeDtypeStruct(block, BF),
-            jax.ShapeDtypeStruct(block, BF),
-            jax.ShapeDtypeStruct((F, F), F32),
+            pltpu.VMEM(block, BF),
+            pltpu.VMEM(block, BF),
+            pltpu.VMEM((F, F), F32),
         ),
         in_specs=[pl.BlockSpec(memory_space=pltpu.HBM)] * 8,
         out_specs=(vmem, vmem, vmem),

time: 102 us -> 98.5 us (0.966)
  the two profiles are of different devices: /device:TPU:1 before, /device:TPU:8 now
where the time goes in v3:
time: 98.5 us; the launch traced here: 98.3 us
  Pallas kernels  95.1 us (97%)
  local copies, waits for them, and re-layouts  1.96 us (2%)
  between operations  1.29 us (1%)
    pallas_call x1, Pallas kernels, per_device(): pl.pallas_call(kernel, out_shape=(pltpu.VMEM(block, BF), pltpu.VMEM(block...  95.1 us

profile of v3, /device:TPU:8, one launch (start us, length us, event | category | flops | bytes accessed | tf_op | source)
XLA Modules:
  0.0 98.3 jit_solution(11723947782459560492)
XLA Ops:
  1.3 95.1 %layer.1 = (bf16[128,256]{1,0:T(8,128)(2,1)S(1)}, bf16[128,256]{1,0:T(8,128)(2,1)S(1)}, f32[256,256]{1,0:T(8,128)S(1)}) custom-call(bf16[128,256]{1,0:T(8,128)(2,1)} %feat_h.1, bf16[256,256]{1,0:T(8,128)(2,1)} %weight_h.1, bf16[128,256]{1,0:T(8,128)(2,1)} %cot_h.1, s32[512,128]{1,0:T(8,128)} %bitcast.5, bf16[128,128,128]{2,1,0:T(8,128)(2,1)} %bitcast.4, ...), custom_call_target="tpu_custom_call" | custom-call | flops 8589934592 | bytes 5242880 | tf_op jit(solution)/shard_map/layer/pallas_call | solution.py:535
  96.4 0.6 copy.14
  97.0 0.6 copy.15
  97.6 0.7 copy.16

commit v4 on v3

--- a/solution.py
+++ b/solution.py
@@ -37,16 +37,17 @@
     ("z", 0, 0, 2, 2), ("c", 3), ("z", 0, 1, 3, 3), ("z", 0, 1, 3, 2),
 )
 SCATTER = (
-    ("c", 4), ("z", 0, 0, 0, 2), ("z", 0, 1, 0, 1), ("z", 0, 1, 0, 3), ("z", 0, 0, 0, 0), ("q", 4),
-    ("c", 3), ("z", 0, 0, 1, 1), ("z", 0, 0, 1, 3), ("q", 3), ("c", 7), ("z", 0, 1, 1, 2),
-    ("z", 0, 1, 1, 0), ("q", 7), ("z", 0, 0, 1, 2), ("z", 0, 1, 1, 1), ("c", 2), ("q", 2), ("w", 0),
-    ("z", 0, 1, 1, 3), ("z", 0, 0, 1, 0), ("c", 6), ("b", 0, 0), ("z", 0, 0, 2, 1), ("q", 6),
-    ("z", 0, 1, 2, 2), ("c", 1), ("z", 0, 0, 2, 3), ("q", 1), ("z", 0, 1, 2, 0), ("c", 5),
-    ("z", 0, 0, 2, 2), ("w", 1), ("q", 5), ("b", 1, 1), ("z", 0, 1, 2, 1), ("z", 0, 0, 2, 0),
-    ("c", 0), ("b", 0, 1), ("z", 0, 1, 2, 3), ("q", 0), ("z", 0, 0, 3, 1), ("z", 0, 1, 3, 2),
-    ("z", 0, 0, 3, 3), ("z", 0, 1, 3, 0), ("w", 2), ("b", 1, 2), ("z", 0, 0, 3, 2),
-    ("z", 0, 1, 3, 1), ("z", 0, 0, 3, 0), ("b", 0, 2), ("z", 0, 1, 3, 3), ("w", 3), ("b", 1, 3),
-    ("y", 0, 2), ("y", 0, 1), ("b", 0, 3), ("y", 0, 3), ("s",), ("t", 0),
+    ("d", 4, 2, 1), ("z", 0, 0, 0, 2), ("z", 0, 1, 0, 1), ("d", 4, 3, 0), ("z", 0, 1, 0, 3),
+    ("z", 0, 0, 0, 0), ("q", 4), ("c", 3), ("z", 0, 0, 1, 1), ("z", 0, 0, 1, 3), ("q", 3), ("c", 7),
+    ("z", 0, 1, 1, 2), ("z", 0, 1, 1, 0), ("q", 7), ("z", 0, 0, 1, 2), ("z", 0, 1, 1, 1), ("c", 2),
+    ("q", 2), ("w", 0), ("z", 0, 1, 1, 3), ("z", 0, 0, 1, 0), ("c", 6), ("b", 0, 0),
+    ("z", 0, 0, 2, 1), ("q", 6), ("z", 0, 1, 2, 2), ("c", 1), ("z", 0, 0, 2, 3), ("q", 1),
+    ("z", 0, 1, 2, 0), ("c", 5), ("z", 0, 0, 2, 2), ("w", 1), ("q", 5), ("b", 1, 1),
+    ("z", 0, 1, 2, 1), ("z", 0, 0, 2, 0), ("c", 0), ("b", 0, 1), ("z", 0, 1, 2, 3), ("q", 0),
+    ("z", 0, 0, 3, 1), ("z", 0, 1, 3, 2), ("z", 0, 0, 3, 3), ("z", 0, 1, 3, 0), ("w", 2),
+    ("b", 1, 2), ("z", 0, 0, 3, 2), ("z", 0, 1, 3, 1), ("z", 0, 0, 3, 0), ("b", 0, 2),
+    ("z", 0, 1, 3, 3), ("w", 3), ("b", 1, 3), ("y", 0, 2), ("y", 0, 1), ("b", 0, 3), ("y", 0, 3),
+    ("s",), ("t", 0),
 )
 CHIP_ORDER = ((1, 2), (1, 1), (1, 3), (1, 0), (0, 2), (0, 1), (0, 3), (0, 0))
 
@@ -120,12 +121,14 @@
 
     sibling = (row, chip * 2 + 1 - core)
 
+    own_line, row_line = col * (NY * NZ) + row, row * (CHIPS * 2) + col
     loads = [
         pltpu.make_async_copy(source, target, in_sem.at[i])
         for i, (source, target) in enumerate(
             (
-                (deg_h, deg), (feat_h, feat), (brow_h, brow), (bcol_h, bcol),
+                (deg_h.at[pl.ds(own_line // 8 * 8, 8)], deg.at[0]), (feat_h, feat), (brow_h, brow), (bcol_h, bcol),
                 (cnt_h, cnt), (weight_h, weight), (cot_h, cot),
+                (deg_h.at[pl.ds(row_line // 8 * 8, 8)], deg.at[1]),
             )
         )
     ]
@@ -142,7 +145,7 @@
 
     for load in loads[:2]:
         load.wait()
-    own_scale = down_rows(scale_of(deg[pl.ds(col * (NY * NZ) + row, 1), :]), F)
+    own_scale = down_rows(scale_of(deg[0, pl.ds(own_line % 8, 1), :]), F)
     src[row] = (feat[...].astype(F32) * own_scale).astype(BF)
 
     pl.semaphore_wait(barrier, len(partners))
@@ -187,12 +190,12 @@
             send(short(r), short(r), hy_s.at[i, d], hy_r.at[i, d], at_y(d))
 
     for c in range(G_PIECES):
-        for way in (0, 1):
-            pass_on(c, way, 0, 0)
-    for c in range(G_PIECES):
         for d in (1, 3, 2):
             i = d * G_PIECES + c
             send(tall(row, c), tall(row, c), gy_s.at[i], gy_r.at[i], at_y(d))
+    for c in range(G_PIECES):
+        for way in (0, 1):
+            pass_on(c, way, 0, 0)
     for way in (0, 1):
         short_pass_on(way, 0)
     short_spread(0, row)
@@ -307,13 +310,13 @@
             if k < CHIPS - 1:
                 chip_out[k] = total.astype(BF)
                 send(chip_out.at[k], chip_in.at[k], chip_s.at[k], chip_r.at[k], at_chip(k))
+    for load in loads[5:]:
+        load.wait()
+    row_scale = down_rows(scale_of(deg[1, pl.ds(row_line % 8, 1), :]), F)
     for k in reversed(range(CHIPS - 1)):
         arrived(chip_in.at[k], chip_r.at[k])
         total = total + chip_in[k].astype(F32)
 
-    for load in loads[5:]:
-        load.wait()
-    row_scale = down_rows(scale_of(deg[pl.ds(row * (CHIPS * 2) + col, 1), :]), F)
     propagated = (total * row_scale).astype(BF)
     pre = jnp.dot(propagated, weight[...], preferred_element_type=F32)
     square = pre * pre
@@ -355,7 +358,7 @@
     for k in reversed(range(CHIPS)):
         arrived(grads.at[chip_from(k) * 2 + 1 - core], fw_r.at[k])
 
-    def back_strip(i):
+    def back_strip(i, ds):
         way, step = strip_way(i)
         z_at = (z + step) % NZ if way == 0 else (z + NZ - step) % NZ
         lhs = jnp.concatenate(
@@ -363,12 +366,13 @@
                 jnp.concatenate(
                     [turned[lookup(r, ((y + d) % NY) * NZ + z_at)] for r in range(16)], axis=1
                 )
-                for d in range(NY)
+                for d in ds
             ],
             axis=0,
         )
         out = jnp.dot(lhs, grads[...].reshape(16 * BS, F), preferred_element_type=F32)
-        part[pl.ds(i * NY, NY)] = out.reshape(NY, BS, F)
+        for j, d in enumerate(ds):
+            part[i * NY + d] = out[j * BS : (j + 1) * BS]
 
     def w_step(step):
         if step == 0:
@@ -417,7 +421,9 @@
 
     for what, *of in SCATTER:
         if what == "c":
-            back_strip(of[0])
+            back_strip(of[0], range(NY))
+        elif what == "d":
+            back_strip(of[0], of[1:])
         elif what == "q":
             i = of[0]
             for d in (2, 1, 3):
@@ -491,7 +497,7 @@
         pltpu.VMEM(block, BF),
         pltpu.VMEM((F, F), BF),
         pltpu.VMEM(block, BF),
-        pltpu.VMEM((512, BS), I32),
+        pltpu.VMEM((2, 8, BS), I32),
         pltpu.VMEM((1, BS), I32),
         pltpu.VMEM((1, BS), I32),
         pltpu.SMEM((1, 1), I32),
@@ -524,7 +530,7 @@
         pltpu.VMEM((2, 4) + low, BF),
         pltpu.VMEM((2, 4) + low, BF),
     ]
-    sems = [dma((7,)), dma, dma]
+    sems = [dma((8,)), dma, dma]
     for shape in (
         (NY * G_PIECES,), (2, 4, NY * G_PIECES), (2,), (CHIPS,), (CHIPS,), (CHIPS,),
         (2, 4, NY * S_PIECES), (NY * S_PIECES,),

time: 98.5 us -> 98 us (level)
  the two profiles are of different devices: /device:TPU:8 before, /device:TPU:1 now
where the time goes in v4:
time: 98 us; the launch traced here: 96.6 us
  Pallas kernels  93.3 us (95%)
  local copies, waits for them, and re-layouts  1.96 us (2%)
  between operations  1.29 us (1%)
    pallas_call x1, Pallas kernels, per_device(): pl.pallas_call(kernel, out_shape=(pltpu.VMEM(block, BF), pltpu.VMEM(block...  93.3 us
    unnamed x3, local copies, waits for them, and re-layouts  1.96 us

profile of v4, /device:TPU:1, one launch (start us, length us, event | category | flops | bytes accessed | tf_op | source)
XLA Modules:
  0.0 96.6 jit_solution(4622421809472097249)
XLA Ops:
  1.3 93.3 %layer.1 = (bf16[128,256]{1,0:T(8,128)(2,1)S(1)}, bf16[128,256]{1,0:T(8,128)(2,1)S(1)}, f32[256,256]{1,0:T(8,128)S(1)}) custom-call(bf16[128,256]{1,0:T(8,128)(2,1)} %feat_h.1, bf16[256,256]{1,0:T(8,128)(2,1)} %weight_h.1, bf16[128,256]{1,0:T(8,128)(2,1)} %cot_h.1, s32[512,128]{1,0:T(8,128)} %bitcast.5, bf16[128,128,128]{2,1,0:T(8,128)(2,1)} %bitcast.4, ...), custom_call_target="tpu_custom_call" | custom-call | flops 8589934592 | bytes 5242880 | tf_op jit(solution)/shard_map/layer/pallas_call | solution.py:541
  94.6 0.6 copy.14
  95.2 0.6 copy.15
  95.9 0.7 copy.16
